TPU v7x, 512 devices: a whole 4x8x8 slice. The times are simulated.
512 devices in a mesh: rows: 128 (over z_hi, x, y), feat: 4 (over z_lo, core).
Axes of the slice: x: 4, y: 8, z: 8 (z_hi: 4, z_lo: 2; z = z_hi * 2 + z_lo), core: 2. Of those that a mesh axis runs over, the one named last changes fastest.
Arguments:
- bin_ids: int32 [128, 262144], P('feat', 'rows'), may hold values from 0 to 255
- node_ids: int32 [262144], P('rows'), may hold values from 0 to 31, as said below
- gradients: bfloat16 [262144], P('rows'), may hold values from -6 to 6
- hessians: bfloat16 [262144], P('rows'), may hold values from 0.099609375 to 1
Outputs:
- gain_table: float32 [128, 32, 256], P('feat')
- best_gain: float32 [32], replicated
Inputs may be any that keep to these rules, and one draw needn't show every extreme that they name: `node_ids`: on some device all 2048 rows lie in one node; on other devices anywhere from none to all rows may lie in one node, and node sizes are very uneven.
All inputs are finite; a program needn't handle non-finite values.
Results may differ from a plain program's by a relative error of at most 0.0003.
Values sent between devices are 32-bit elements; how exact they have to be, the bound alone decides.
A program may use at most 64 MiB of HBM per device.

v0:
```python
import jax
import jax.numpy as jnp
from jax import lax
from jax.sharding import PartitionSpec as P

BINS = 256
NODES = 32


def gains_of(packed, width):
    grad_hist = packed[:, :width]
    hess_hist = packed[:, width:]
    left_grad = jnp.cumsum(grad_hist, axis=-1)
    left_hess = jnp.cumsum(hess_hist, axis=-1)
    total_grad = jnp.sum(grad_hist, axis=-1, keepdims=True)
    total_hess = jnp.sum(hess_hist, axis=-1, keepdims=True)
    lam = jnp.float32(1.0)
    right_grad = total_grad - left_grad
    right_hess = total_hess - left_hess
    return (
        left_grad * left_grad / (left_hess + lam)
        + right_grad * right_grad / (right_hess + lam)
        - total_grad * total_grad / (total_hess + lam)
    )


def histogram(sub_bins, weighted, width):
    feats, count_rows = sub_bins.shape
    block = min(512, count_rows)
    steps = count_rows // block
    bin_blocks = sub_bins.reshape(feats, steps, block).transpose(1, 0, 2)
    weight_blocks = weighted.reshape(steps, block, weighted.shape[1])
    levels = lax.broadcasted_iota(jnp.int32, (1, 1, width), 2)

    def accumulate(total, pair):
        bins_here, weights_here = pair
        onehot = (bins_here[:, :, None] == levels).astype(jnp.bfloat16)
        return (
            total
            + jnp.einsum("rc,frb->cfb", weights_here, onehot, preferred_element_type=jnp.float32),
            None,
        )

    start_total = jnp.zeros((weighted.shape[1], feats, width), jnp.float32)
    total, unused = lax.scan(accumulate, start_total, (bin_blocks, weight_blocks))
    return total


def pack_pairs(hist, node_span, feat_span, width):
    return (
        hist.reshape(2, node_span, feat_span, width)
        .transpose(2, 1, 0, 3)
        .reshape(feat_span * node_span, 2 * width)
    )


def best_from_table(table):
    return lax.pmax(jnp.max(table, axis=(0, 2)), "feat")


def per_device(bin_ids, node_ids, gradients, hessians):
    feats = bin_ids.shape[0]
    node_count = NODES
    width = BINS
    pair_rows = feats * node_count
    node_levels = lax.broadcasted_iota(jnp.int32, (1, node_count), 1)
    node_hot = (node_ids[:, None] == node_levels).astype(jnp.bfloat16)
    weighted = jnp.concatenate(
        [node_hot * gradients[:, None], node_hot * hessians[:, None]], axis=1
    )
    own_rows = pair_rows // lax.axis_size("rows")
    span = own_rows * lax.axis_size("rows") // node_count
    share = lax.psum_scatter(
        pack_pairs(histogram(bin_ids, weighted, width), node_count, span, width),
        "rows",
        scatter_dimension=0,
        tiled=True,
    )
    share_gain = gains_of(share, width)
    table = lax.all_gather(share_gain, "rows", axis=0, tiled=True).reshape(feats, node_count, width)
    best_gain = best_from_table(table)
    return (table, best_gain)


def solution(mesh):
    in_specs = (P("feat", "rows"), P("rows"), P("rows"), P("rows"))
    out_specs = (P("feat", None, None), P())
    return jax.shard_map(
        per_device, mesh=mesh, in_specs=in_specs, out_specs=out_specs, check_vma=False
    )
```

profile of v0, /device:TPU:1, one launch (start us, length us, event | category | flops | bytes accessed | tf_op | source)
XLA Modules:
  0.0 945.4 jit_solution(9553876471919173964)
XLA Ops:
  7.2 0.0 reduce-scatter.2.cloned.1.call-start
  7.2 0.7 eq.34
  7.9 0.7 mul.34
  8.6 0.7 mul.37
  9.3 1.1 reshape.82
  10.5 38.4 %while.11 = (s32[]{:T(128)}, f32[64,32,256]{2,0,1:T(8,128)S(1)}, bf16[4,512,64]{1,2,0:T(8,128)(2,1)S(1)}, s32[4,32,512]{2,0,1:T(4,128)S(1)}, s32[]{:T(128)}, /*index=5*/s32[]{:T(128)}) while((s32[]{:T(128)}, f32[64,32,256]{2,0,1:T(8,128)S(1)}, bf16[4,512,64]{1,2,0:T(8,128)(2,1)S(1)}, s32[4,32,512]{2,0,1:T(4,128)S(1)}, s32[]{:T(128)}, ...), condition=%wide.region_1.2_spmd.clone, body=%wide.region_0.1_spmd.clone.sunk | while | flops 542113792 | bytes 4587607 | solution.py:45
  10.5 0.1 constant_dynamic-slice_fusion.2
  10.6 9.5 %select_add_fusion.2 = f32[64,32,256]{2,0,1:T(8,128)S(1)} fusion(f32[64,32,256]{2,0,1:T(8,128)S(1)} %get-tuple-element.101, s32[32,512]{1,0:T(8,128)S(1)} %bitcast.50, pred[]{:T(512)S(6)} %compare.3, bf16[4,512,64]{1,2,0:T(8,128)(2,1)S(1)} %get-tuple-element.108, s32[]{:T(128)} %get-tuple-element.100), kind=kOutput, calls=%fused_computation.4.clone.1 | convolution fusion | flops 542113792 | bytes 4325381 | tf_op jit(solution)/shard_map/while/body/eval_jaxpr/rc,frb->cfb/dot_general | solution.py:40
  20.1 0.1 constant_dynamic-slice_fusion.2
  20.2 9.5 %select_add_fusion.2 = f32[64,32,256]{2,0,1:T(8,128)S(1)} fusion(f32[64,32,256]{2,0,1:T(8,128)S(1)} %get-tuple-element.101, s32[32,512]{1,0:T(8,128)S(1)} %bitcast.50, pred[]{:T(512)S(6)} %compare.3, bf16[4,512,64]{1,2,0:T(8,128)(2,1)S(1)} %get-tuple-element.108, s32[]{:T(128)} %get-tuple-element.100), kind=kOutput, calls=%fused_computation.4.clone.1 | convolution fusion | flops 542113792 | bytes 4325381 | tf_op jit(solution)/shard_map/while/body/eval_jaxpr/rc,frb->cfb/dot_general | solution.py:40
  29.8 0.1 constant_dynamic-slice_fusion.2
  29.8 9.5 %select_add_fusion.2 = f32[64,32,256]{2,0,1:T(8,128)S(1)} fusion(f32[64,32,256]{2,0,1:T(8,128)S(1)} %get-tuple-element.101, s32[32,512]{1,0:T(8,128)S(1)} %bitcast.50, pred[]{:T(512)S(6)} %compare.3, bf16[4,512,64]{1,2,0:T(8,128)(2,1)S(1)} %get-tuple-element.108, s32[]{:T(128)} %get-tuple-element.100), kind=kOutput, calls=%fused_computation.4.clone.1 | convolution fusion | flops 542113792 | bytes 4325381 | tf_op jit(solution)/shard_map/while/body/eval_jaxpr/rc,frb->cfb/dot_general | solution.py:40
  39.4 0.1 constant_dynamic-slice_fusion.2
  39.5 9.5 %select_add_fusion.2 = f32[64,32,256]{2,0,1:T(8,128)S(1)} fusion(f32[64,32,256]{2,0,1:T(8,128)S(1)} %get-tuple-element.101, s32[32,512]{1,0:T(8,128)S(1)} %bitcast.50, pred[]{:T(512)S(6)} %compare.3, bf16[4,512,64]{1,2,0:T(8,128)(2,1)S(1)} %get-tuple-element.108, s32[]{:T(128)} %get-tuple-element.100), kind=kOutput, calls=%fused_computation.4.clone.1 | convolution fusion | flops 542113792 | bytes 4325381 | tf_op jit(solution)/shard_map/while/body/eval_jaxpr/rc,frb->cfb/dot_general | solution.py:40
  49.0 1.7 copy.9
  50.7 1.5 copy.11
  52.2 0.0 reduce-scatter.2.cloned.1.call-update
  52.2 0.0 all-gather.2.cloned.1.call-start
  52.3 660.5 %reduce-scatter.2.cloned.1.call-done = f32[8,512]{1,0:T(8,128)} async-done(((f32[1024,512]{1,0:T(8,128)}), f32[8,512]{1,0:T(8,128)}) %reduce-scatter.2.cloned.1.call-update) | async-done | bytes 16400 | tf_op jit(solution)/shard_map/reduce_scatter | solution.py:73
  712.7 0.9 slice_reduce_fusion.3
  713.6 0.6 reduce-window.14
  714.2 0.2 slice_reduce_fusion.1
  714.4 0.6 reduce-window.16
  715.0 0.2 slice_reduce_fusion
  715.2 0.7 fusion.11
  715.9 0.0 all-gather.2.cloned.1.call-update
  715.9 209.1 %all-gather.2.cloned.1.call-done = f32[1024,256]{1,0:T(8,128)} async-done(((f32[8,256]{1,0:T(8,128)}), f32[1024,256]{1,0:T(8,128)}) %all-gather.2.cloned.1.call-update) | async-done | bytes 1048592 | tf_op jit(solution)/shard_map/all_gather | solution.py:80
  925.0 1.4 reduce_max.10
  926.5 0.1 reduce_max.14
  926.6 9.7 %pmax.7 = f32[32]{0:T(128)} all-reduce(f32[32]{0:T(128)S(1)} %reduce_max.18), channel_id=1, replica_groups=mesh['rows'=128,'feat'=4] {'feat'}, use_global_device_ids=true, to_apply=%region_11.12 | all-reduce | flops 32 | bytes 256 | tf_op jit(solution)/shard_map/pmax | solution.py:58
  936.2 2.3 copy.23
  (13 shorter events, 0.2 us)
Async XLA Ops:
  7.2 705.6 %reduce-scatter.2.cloned.1.call-start = ((), (), s32[]{:S(2)}) async-start(), calls=%async_computation.1 | async-start | bytes 2113536 | tf_op jit(solution)/shard_map/reduce_scatter | solution.py:73
  52.2 872.8 %all-gather.2.cloned.1.call-start = ((), (), s32[]{:S(2)}) async-start(), calls=%async_computation.2 | async-start | bytes 1056768 | tf_op jit(solution)/shard_map/all_gather | solution.py:80
Sparse Core Ops, SparseCore 0:
  52.3 660.3 reduce-scatter.1
  718.5 206.4 all-gather.1
where the time goes:
time: 946 us; the launch traced here: 945 us
  waiting for transfers between devices  870 us (92%)
  matrix products  38 us (4%)
  between operations  14.1 us (1%)
  blocking collectives  9.66 us (1%)
    reduce_scatter x1, waiting for transfers between devices, per_device(): lax.psum_scatter(pack_pairs(histogram(bin_ids, weighted, width), node_cou...  660 us
    all_gather x1, waiting for transfers between devices, per_device(): lax.all_gather(share_gain, 'rows', axis=0, tiled=True)  209 us
    dot_general x4, matrix products, accumulate(): jnp.einsum('rc,frb->cfb', weights_here, onehot, preferred_element_type=jn...  38 us
  transfers between devices with their start and end apart: 2, of which 2 were waited for; matrix products, arithmetic and copies ran while one was open for 0% of the time, Pallas kernels for 0%

commit v1 on v0

v1 whole, which is shorter than its diff:
```python
import functools

import jax
import jax.numpy as jnp
from jax import lax
from jax.experimental import pallas as pl
from jax.experimental.pallas import tpu as pltpu
from jax.sharding import PartitionSpec as P

MESH = pl.DeviceIdType.MESH
BINS = 256
NODES = 32
HALF = 128
NX, NY, NZ = 4, 8, 4
NF = 8
ROWS = 2048
CH = 2 * NODES
QUARTER = 2 * NODES // NZ


def build_weights(aux, weights, slot):
    row = lax.broadcasted_iota(jnp.int32, (CH, HALF), 0)
    node_of = ((row // QUARTER) * 8 + row % 8).astype(jnp.float32)
    is_grad = (row % QUARTER) < 8
    for i in range(ROWS // HALF):
        node = jnp.broadcast_to(aux[slot, 0, i : i + 1, :], (CH, HALF))
        grad = jnp.broadcast_to(aux[slot, 1, i : i + 1, :], (CH, HALF))
        hess = jnp.broadcast_to(aux[slot, 2, i : i + 1, :], (CH, HALF))
        value = jnp.where(node == node_of, jnp.where(is_grad, grad, hess), 0.0)
        weights[slot, :, i * HALF : (i + 1) * HALF] = value.astype(jnp.bfloat16)


def partial_hist(bins, weights, levels, slot, feature):
    ids = bins[slot, pl.ds(feature, 1), :]
    high = jnp.broadcast_to(ids >= HALF, (CH, ROWS))
    low = (ids & (HALF - 1)).astype(jnp.float32).astype(jnp.bfloat16)
    w = weights[slot]
    zero = jnp.zeros_like(w)
    left = jnp.concatenate([jnp.where(high, zero, w), jnp.where(high, w, zero)], axis=0)
    hot = jnp.where(jnp.broadcast_to(low, (HALF, ROWS)) == levels, jnp.bfloat16(1), jnp.bfloat16(0))
    return lax.dot_general(left, hot, (((1,), (1,)), ((), ())), preferred_element_type=jnp.float32)


def side_by_side(d):
    return jnp.concatenate([d[:CH], d[CH:]], axis=1)


def prefix_sums(values):
    r = lax.broadcasted_iota(jnp.int32, (BINS, BINS), 0)
    c = lax.broadcasted_iota(jnp.int32, (BINS, BINS), 1)
    upto = jnp.where(r <= c, 1.0, 0.0).astype(jnp.bfloat16)
    first = values.astype(jnp.bfloat16)
    rest = values - first.astype(jnp.float32)
    second = rest.astype(jnp.bfloat16)
    third = (rest - second.astype(jnp.float32)).astype(jnp.bfloat16)
    n = values.shape[0]
    parts = jnp.concatenate([first.astype(jnp.float32), second.astype(jnp.float32), third.astype(jnp.float32)], axis=0)
    sums = jnp.dot(parts.astype(jnp.bfloat16), upto, preferred_element_type=jnp.float32)
    left = (sums[2 * n :] + sums[n : 2 * n]) + sums[:n]
    total = jnp.broadcast_to(left[:, BINS - 1 :], left.shape)
    return left, total


def kernel(bins_hbm, aux_hbm, table, best,
           bins, aux, weights, acc, inbox_y, mine, inbox_z, tops,
           local_sems, a_send, a_recv, w_send, w_recv, y_send, y_recv, z_send, z_recv,
           gz_send, gz_recv, gy_send, gy_recv, gx_send, gx_recv, f_send, f_recv, ready):
    r = lax.axis_index("rows")
    f = lax.axis_index("feat")
    zh, x, y = r // (NX * NY), (r // NY) % NX, r % NY
    zl, core = f // 2, f % 2

    def at(dz, dx, dy, dzl=0, dc=0):
        row = (((zh + dz) % NZ) * NX + (x + dx) % NX) * NY + (y + dy) % NY
        return (row, ((zl + dzl) % 2) * 2 + (core + dc) % 2)

    def remote(src, dst, send, recv, to):
        return pltpu.make_async_remote_copy(src_ref=src, dst_ref=dst, send_sem=send, recv_sem=recv, device_id=to, device_id_type=MESH)

    barrier = pltpu.get_barrier_semaphore()
    near = [at(0, 1, 0), at(0, 2, 0), at(0, 3, 0), at(0, 0, 1), at(0, 0, 2), at(0, 0, 6), at(0, 0, 7),
            at(1, 0, 0), at(3, 0, 0), at(0, 0, 0, 1, 0), at(0, 0, 0, 0, 1), at(0, 0, 0, 1, 1)]
    for to in near:
        pl.semaphore_signal(barrier, inc=1, device_id=to, device_id_type=MESH)

    own_bins = pltpu.make_async_copy(bins_hbm.at[pl.ds(pl.multiple_of(x * NF, NF), NF)], bins.at[0], local_sems.at[0])
    own_aux = pltpu.make_async_copy(aux_hbm, aux.at[0], local_sems.at[1])
    own_bins.start()
    own_aux.start()
    pl.semaphore_wait(barrier, len(near))

    exchange = []
    for d in (2, 1, 3):
        to = at(0, d, 0)
        start = pl.multiple_of(((x + d) % NX) * NF, NF)
        exchange.append(remote(aux_hbm, aux.at[d], w_send.at[d], w_recv.at[d], to))
        exchange.append(remote(bins_hbm.at[pl.ds(start, NF)], bins.at[d], a_send.at[d], a_recv.at[d], to))
    for copy in exchange:
        copy.start()
    for to in (at(0, 0, 2), at(0, 0, 6), at(1, 0, 0), at(3, 0, 0)):
        pl.semaphore_signal(ready, inc=1, device_id=to, device_id_type=MESH)

    levels = lax.broadcasted_iota(jnp.int32, (HALF, ROWS), 0).astype(jnp.float32).astype(jnp.bfloat16)
    own_aux.wait()
    own_bins.wait()
    build_weights(aux, weights, 0)

    @pl.loop(0, NF, unroll=4)
    def _(j):
        acc[j] = side_by_side(partial_hist(bins, weights, levels, 0, j))

    for copy in exchange:
        copy.wait()
    for s in (1, 3, 2):
        build_weights(aux, weights, s)
    pl.semaphore_wait(ready, 4)

    @pl.loop(0, NF, unroll=2)
    def _(i):
        m = (i + 1) // 2
        k = (NY // 2 + m * (1 - 2 * (i % 2))) % NY
        j = (y + k) % NY
        d = partial_hist(bins, weights, levels, 1, j)
        d += partial_hist(bins, weights, levels, 3, j)
        d += partial_hist(bins, weights, levels, 2, j)
        acc[j] = acc[j] + side_by_side(d)

        @pl.when(i < NF - 1)
        def _():
            remote(acc.at[j], inbox_y.at[k], y_send.at[k], y_recv.at[k], at(0, 0, k)).start()

    total = acc[y]
    for k in (4, 3, 5, 2, 6, 1, 7):
        copy = remote(acc.at[0], inbox_y.at[k], y_send.at[k], y_recv.at[k], at(0, 0, k))
        copy.wait_recv()
        total = total + inbox_y[k]
    mine[...] = total

    copies = []
    for d in (2, 1, 3):
        q = (zh + d) % NZ
        copy = remote(mine.at[pl.ds(pl.multiple_of(q * QUARTER, QUARTER), QUARTER)], inbox_z.at[d], z_send.at[d], z_recv.at[d], at(d, 0, 0))
        copy.start()
        copies.append(copy)
    hist = mine[pl.ds(pl.multiple_of(zh * QUARTER, QUARTER), QUARTER), :]
    for copy, d in zip(copies, (2, 1, 3)):
        copy.wait_recv()
        hist = hist + inbox_z[d]

    left, whole = prefix_sums(hist)
    lg, lh, tg, th = left[:8], left[8:], whole[:8], whole[8:]
    rg, rh = tg - lg, th - lh
    gains = lg * lg / (lh + 1.0) + rg * rg / (rh + 1.0) - tg * tg / (th + 1.0)

    me = x * NF + y
    rows = pl.ds(pl.multiple_of(zh * 8, 8), 8)
    table[me, rows, :] = gains

    gathers = []
    for d in (2, 1, 3):
        copy = remote(table.at[me, rows], table.at[me, rows], gz_send.at[d], gz_recv.at[d], at(d, 0, 0))
        copy.start()
        gathers.append(copy)
    for copy in gathers:
        copy.wait_recv()

    sent = list(gathers)
    arrive = {}
    for k in (4, 3, 5, 2, 6, 1, 7):
        copy = remote(table.at[me], table.at[me], gy_send.at[k], gy_recv.at[k], at(0, 0, k))
        copy.start()
        sent.append(copy)
        arrive[k] = copy
    last = []
    for k in (0, 1, 7, 2, 6, 3, 5, 4):
        if k:
            arrive[k].wait_recv()
        here = x * NF + (y + NY - k) % NY
        for d in (2, 1, 3):
            copy = remote(table.at[here], table.at[here], gx_send.at[d, k], gx_recv.at[d, k], at(0, d, 0))
            copy.start()
            sent.append(copy)
            last.append(copy)
    for copy in last:
        copy.wait_recv()

    top = jnp.max(table[...], axis=0)
    tops[0] = jnp.broadcast_to(jnp.max(top, axis=1, keepdims=True), (NODES, HALF))
    fins = []
    for n, (dzl, dc) in enumerate(((1, 0), (0, 1), (1, 1)), 1):
        copy = remote(tops.at[0], tops.at[n], f_send.at[n], f_recv.at[n], at(0, 0, 0, dzl, dc))
        copy.start()
        fins.append(copy)
    for copy in sent:
        copy.wait_send()
    for copy in copies:
        copy.wait_send()
    for k in range(1, NY):
        remote(acc.at[0], inbox_y.at[k], y_send.at[k], y_recv.at[k], at(0, 0, k)).wait_send()
    for copy in fins:
        copy.wait()
    over = jnp.maximum(jnp.maximum(tops[0], tops[1]), jnp.maximum(tops[2], tops[3]))
    lane = lax.broadcasted_iota(jnp.int32, (NODES, HALF), 1)
    node = lax.broadcasted_iota(jnp.int32, (NODES, HALF), 0)
    best[...] = jnp.max(jnp.where(lane == node, over, -jnp.inf), axis=0, keepdims=True)


def per_device(bin_ids, node_ids, gradients, hessians):
    f32 = jnp.float32
    aux = jnp.stack([node_ids.astype(f32), gradients.astype(f32), hessians.astype(f32)]).reshape(3, ROWS // HALF, HALF)
    dma = pltpu.SemaphoreType.DMA
    table, best = pl.pallas_call(
        kernel,
        out_shape=(
            jax.ShapeDtypeStruct((NX * NF, NODES, BINS), f32),
            jax.ShapeDtypeStruct((1, HALF), f32),
        ),
        in_specs=[pl.BlockSpec(memory_space=pl.ANY)] * 2,
        out_specs=(pl.BlockSpec(memory_space=pltpu.VMEM), pl.BlockSpec(memory_space=pltpu.VMEM)),
        scratch_shapes=[
            pltpu.VMEM((NX, NF, ROWS), jnp.int32),
            pltpu.VMEM((NX, 3, ROWS // HALF, HALF), f32),
            pltpu.VMEM((NX, CH, ROWS), jnp.bfloat16),
            pltpu.VMEM((NF, CH, BINS), f32),
            pltpu.VMEM((NY, CH, BINS), f32),
            pltpu.VMEM((CH, BINS), f32),
            pltpu.VMEM((NZ, QUARTER, BINS), f32),
            pltpu.VMEM((4, NODES, HALF), f32),
            dma((2,)),
            dma((NX,)), dma((NX,)),
            dma((NX,)), dma((NX,)),
            dma((NY,)), dma((NY,)),
            dma((NZ,)), dma((NZ,)),
            dma((NZ,)), dma((NZ,)),
            dma((NY,)), dma((NY,)),
            dma((NX, NY)), dma((NX, NY)),
            dma((4,)), dma((4,)),
            pltpu.SemaphoreType.REGULAR,
        ],
        compiler_params=pltpu.CompilerParams(collective_id=0, has_side_effects=True, vmem_limit_bytes=40 * 2**20),
        cost_estimate=pl.CostEstimate(flops=2 * 32 * ROWS * CH * BINS, bytes_accessed=2 * 2**20, transcendentals=0),
        name="split_gains",
    )(bin_ids, aux)
    return table, best[0, :NODES]


def solution(mesh):
    in_specs = (P("feat", "rows"), P("rows"), P("rows"), P("rows"))
    out_specs = (P("feat", None, None), P())
    return jax.shard_map(per_device, mesh=mesh, in_specs=in_specs, out_specs=out_specs, check_vma=False)
```

time: 946 us -> 66.1 us (0.07)
  waiting for transfers between devices: 870 us -> 0 us
  Pallas kernels: 0 us -> 62 us
  matrix products: 38 us -> 0 us
  between operations: 14.1 us -> 0.68 us
  blocking collectives: 9.66 us -> 0 us
    reduce_scatter x1 -> x0, waiting for transfers between devices: 660 us -> none  [per_device(): lax.psum_scatter(pack_pairs(histogram(bin_ids, weighted, width), node_cou...]
    all_gather x1 -> x0, waiting for transfers between devices: 209 us -> none  [per_device(): lax.all_gather(share_gain, 'rows', axis=0, tiled=True)]
    pallas_call x0 -> x1, Pallas kernels: none -> 62 us  [per_device(): pl.pallas_call(kernel, out_shape=(jax.ShapeDtypeStruct((NX * NF, NODES, B...]
    dot_general x4 -> x0, matrix products: 38 us -> none  [accumulate(): jnp.einsum('rc,frb->cfb', weights_here, onehot, preferred_element_type=jn...]
    pmax x1 -> x0, blocking collectives: 9.66 us -> none  [best_from_table(): return lax.pmax(jnp.max(table, axis=(0, 2)), 'feat')]
  transfers between devices with their start and end apart: 2 -> 0, of which waited for: 2 -> 0; matrix products, arithmetic and copies ran while one was open for 0% -> 0% of each run, Pallas kernels for 0% -> 0%
where the time goes in v1:
time: 66.1 us; the launch traced here: 65.9 us
  Pallas kernels  62 us (94%)
  local copies, waits for them, and re-layouts  2.44 us (4%)
  other arithmetic  0.72 us (1%)
  between operations  0.68 us (1%)
    pallas_call x1, Pallas kernels, per_device(): pl.pallas_call(kernel, out_shape=(jax.ShapeDtypeStruct((NX * NF, NODES, B...  62 us
    unnamed x7, local copies, waits for them, and re-layouts  1.92 us

profile of v1, /device:TPU:1, one launch (start us, length us, event | category | flops | bytes accessed | tf_op | source)
XLA Modules:
  0.0 65.9 jit_solution(296134921665085762)
XLA Ops:
  0.6 0.0 copy-start.1
  0.6 0.0 copy-start.2
  0.7 0.7 %convert_bitcast_fusion = f32[1,16,128]{2,1,0:T(8,128)S(1)} fusion(s32[2048]{0:T(1024)} %param.5), kind=kLoop, calls=%fused_computation.1 | loop fusion | flops 2048 | bytes 16384 | tf_op jit(solution)/shard_map/stack | solution.py:210
  1.4 0.0 copy-done.1
  1.4 0.0 copy-done.2
  1.4 0.0 copy-start
  1.4 0.9 %copy-done = s32[32,2048]{1,0:T(8,128)S(1)} copy-done((s32[32,2048]{1,0:T(8,128)S(1)}, s32[32,2048]{1,0:T(8,128)}, u32[]{:S(2)}) %copy-start) | copy-done | bytes 262168
  2.3 62.0 %split_gains.1 = (f32[32,32,256]{2,1,0:T(8,128)S(1)}, f32[1,128]{1,0:T(1,128)S(1)}) custom-call(s32[32,2048]{1,0:T(8,128)S(1)} %copy-done, f32[3,16,128]{2,1,0:T(8,128)S(1)} %pad_maximum_fusion.aux_hbm), custom_call_target="tpu_custom_call" | custom-call | flops 2147483648 | bytes 2097152 | tf_op jit(solution)/shard_map/split_gains/pallas_call | solution.py:212
  64.4 0.5 slice_bitcast_fusion
  64.9 1.0 %copy.7 = f32[32,32,256]{2,1,0:T(8,128)} copy(f32[32,32,256]{2,1,0:T(8,128)S(1)} %get-tuple-element.10) | data formatting | bytes 2097152
  (2 shorter events, 0.0 us)
Async XLA Ops:
  0.6 0.7 %copy-start.1 = (bf16[2048]{0:T(1024)(128)(2,1)S(1)}, bf16[2048]{0:T(1024)(128)(2,1)}, u32[]{:S(2)}) copy-start(bf16[2048]{0:T(1024)(128)(2,1)} %param.7) | copy-start | bytes 12292
  0.6 0.7 %copy-start.2 = (bf16[2048]{0:T(1024)(128)(2,1)S(1)}, bf16[2048]{0:T(1024)(128)(2,1)}, u32[]{:S(2)}) copy-start(bf16[2048]{0:T(1024)(128)(2,1)} %param.6) | copy-start | bytes 12292
  1.4 1.0 %copy-start = (s32[32,2048]{1,0:T(8,128)S(1)}, s32[32,2048]{1,0:T(8,128)}, u32[]{:S(2)}) copy-start(s32[32,2048]{1,0:T(8,128)} %bins_hbm.1) | copy-start | bytes 786436

commit v2 on v1

v2 whole, which is shorter than its diff:
```python
import functools

import jax
import jax.numpy as jnp
from jax import lax
from jax.experimental import pallas as pl
from jax.experimental.pallas import tpu as pltpu
from jax.sharding import PartitionSpec as P

MESH = pl.DeviceIdType.MESH
BINS = 256
NODES = 32
HALF = 128
NX, NY, NZ = 4, 8, 4
NG = 4
ROWS = 2048
CH = 2 * NODES
QUARTER = 2 * NODES // NZ


def build_weights(aux, weights, slot):
    row = lax.broadcasted_iota(jnp.int32, (CH, HALF), 0)
    node_of = ((row // QUARTER) * 8 + row % 8).astype(jnp.float32)
    is_grad = (row % QUARTER) < 8
    for i in range(ROWS // HALF):
        node = jnp.broadcast_to(aux[slot, 0, i : i + 1, :], (CH, HALF))
        grad = jnp.broadcast_to(aux[slot, 1, i : i + 1, :], (CH, HALF))
        hess = jnp.broadcast_to(aux[slot, 2, i : i + 1, :], (CH, HALF))
        value = jnp.where(node == node_of, jnp.where(is_grad, grad, hess), 0.0)
        weights[slot, :, i * HALF : (i + 1) * HALF] = value.astype(jnp.bfloat16)


def partial_hist(bins, weights, levels, slot, feature):
    ids = bins[slot, pl.ds(feature, 1), :]
    high = jnp.broadcast_to(ids >= HALF, (CH, ROWS))
    low = (ids & (HALF - 1)).astype(jnp.float32).astype(jnp.bfloat16)
    w = weights[slot]
    zero = jnp.zeros_like(w)
    left = jnp.concatenate([jnp.where(high, zero, w), jnp.where(high, w, zero)], axis=0)
    hot = jnp.where(jnp.broadcast_to(low, (HALF, ROWS)) == levels, jnp.bfloat16(1), jnp.bfloat16(0))
    return lax.dot_general(left, hot, (((1,), (1,)), ((), ())), preferred_element_type=jnp.float32)


def side_by_side(d):
    return jnp.concatenate([d[:CH], d[CH:]], axis=1)


def prefix_sums(values):
    r = lax.broadcasted_iota(jnp.int32, (BINS, BINS), 0)
    c = lax.broadcasted_iota(jnp.int32, (BINS, BINS), 1)
    upto = jnp.where(r <= c, 1.0, 0.0).astype(jnp.bfloat16)
    first = values.astype(jnp.bfloat16)
    rest = values - first.astype(jnp.float32)
    second = rest.astype(jnp.bfloat16)
    third = (rest - second.astype(jnp.float32)).astype(jnp.bfloat16)
    n = values.shape[0]
    parts = jnp.concatenate([first.astype(jnp.float32), second.astype(jnp.float32), third.astype(jnp.float32)], axis=0)
    sums = jnp.dot(parts.astype(jnp.bfloat16), upto, preferred_element_type=jnp.float32)
    left = (sums[2 * n :] + sums[n : 2 * n]) + sums[:n]
    total = jnp.broadcast_to(left[:, BINS - 1 :], left.shape)
    return left, total


def kernel(bins_hbm, aux_hbm, table, best,
           bins, aux, weights, acc, inbox, tops,
           local_sems, a_send, a_recv, w_send, w_recv, h_send, h_recv,
           g_send, g_recv, x_send, x_recv, f_send, f_recv, ready):
    r = lax.axis_index("rows")
    f = lax.axis_index("feat")
    zh, x, y = r // (NX * NY), (r // NY) % NX, r % NY
    zl, core = f // 2, f % 2
    yh, yl = y // 2, y % 2

    def at(dz, dx, dy, dzl=0, dc=0):
        row = (((zh + dz) % NZ) * NX + (x + dx) % NX) * NY + (y + dy) % NY
        return (row, ((zl + dzl) % 2) * 2 + (core + dc) % 2)

    def pair(dx, p):
        return at(0, dx, (1 - 2 * yl) * p)

    def remote(src, dst, send, recv, to):
        return pltpu.make_async_remote_copy(src_ref=src, dst_ref=dst, send_sem=send, recv_sem=recv, device_id=to, device_id_type=MESH)

    barrier = pltpu.get_barrier_semaphore()
    near = [pair(2, 1), pair(1, 1), pair(3, 1), at(0, 2, 0), at(0, 1, 0), at(0, 3, 0),
            at(0, 0, 2), at(0, 0, 6), at(1, 0, 0), at(3, 0, 0), at(0, 0, 1), at(0, 0, 7),
            at(0, 0, 0, 1, 0), at(0, 0, 0, 0, 1), at(0, 0, 0, 1, 1)]
    for to in near:
        pl.semaphore_signal(barrier, inc=1, device_id=to, device_id_type=MESH)

    def features_of(dx, p):
        group = ((x + dx) % NX) * 2 + (yl + p) % 2
        return pl.ds(group * NG, NG)

    own_bins = pltpu.make_async_copy(bins_hbm.at[features_of(0, 0)], bins.at[0], local_sems.at[0])
    own_aux = pltpu.make_async_copy(aux_hbm, aux.at[0], local_sems.at[1])
    own_bins.start()
    own_aux.start()
    pl.semaphore_wait(barrier, len(near))

    exchange = {}
    for dx, p in ((1, 0), (3, 0), (0, 1), (2, 0), (1, 1), (3, 1), (2, 1)):
        s = dx * 2 + p
        to = pair(dx, p)
        exchange[s] = (
            remote(aux_hbm, aux.at[s], w_send.at[s], w_recv.at[s], to),
            remote(bins_hbm.at[features_of(dx, p)], bins.at[s], a_send.at[s], a_recv.at[s], to),
        )
        for copy in exchange[s]:
            copy.start()
    for to in (at(0, 0, 2), at(0, 0, 6), at(1, 0, 0), at(3, 0, 0)):
        pl.semaphore_signal(ready.at[0], inc=1, device_id=to, device_id_type=MESH)

    levels = lax.broadcasted_iota(jnp.int32, (HALF, ROWS), 0).astype(jnp.float32).astype(jnp.bfloat16)
    own_aux.wait()
    own_bins.wait()
    build_weights(aux, weights, 0)

    @pl.loop(0, NG, unroll=4)
    def _(j):
        acc[j] = side_by_side(partial_hist(bins, weights, levels, 0, j))

    pl.semaphore_wait(ready.at[0], 4)
    for d in (2, 1, 3):
        pl.semaphore_signal(ready.at[1], inc=1, device_id=at(d, 0, 0), device_id_type=MESH)

    for s in (2, 6, 1):
        for copy in exchange[s]:
            copy.wait()
        build_weights(aux, weights, s)

        @pl.loop(0, NG, unroll=4)
        def _(j):
            acc[j] = acc[j] + side_by_side(partial_hist(bins, weights, levels, s, j))

    for s in (4, 3, 7, 5):
        for copy in exchange[s]:
            copy.wait()
        build_weights(aux, weights, s)
    pl.semaphore_wait(ready.at[1], 3)

    @pl.loop(0, NG, unroll=2)
    def _(i):
        m = (i + 1) // 2
        a = (2 + m * (1 - 2 * (i % 2))) % 4
        j = (yh + a) % 4
        d = partial_hist(bins, weights, levels, 4, j)
        for s in (3, 7, 5):
            d += partial_hist(bins, weights, levels, s, j)
        acc[j] = acc[j] + side_by_side(d)
        for b in (2, 1, 3, 0):
            quarter = pl.ds(pl.multiple_of(((zh + b) % NZ) * QUARTER, QUARTER), QUARTER)

            @pl.when(a + b > 0)
            def _():
                remote(acc.at[j, quarter], inbox.at[a, b], h_send.at[a, b], h_recv.at[a, b], at(b, 0, 2 * a)).start()

    hist = acc[yh, pl.ds(pl.multiple_of(zh * QUARTER, QUARTER), QUARTER), :]
    others = [(a, b) for a in (0, 1, 3, 2) for b in (0, 1, 3, 2) if a or b]
    for a, b in others:
        remote(acc.at[0, pl.ds(0, QUARTER)], inbox.at[a, b], h_send.at[a, b], h_recv.at[a, b], at(b, 0, 2 * a)).wait_recv()
        hist = hist + inbox[a, b]

    left, whole = prefix_sums(hist)
    lg, lh, tg, th = left[:8], left[8:], whole[:8], whole[8:]
    rg, rh = tg - lg, th - lh
    gains = lg * lg / (lh + 1.0) + rg * rg / (rh + 1.0) - tg * tg / (th + 1.0)

    def feature_at(dy):
        there = (y + dy) % NY
        return (x * 2 + there % 2) * NG + there // 2

    me = feature_at(0)
    rows = pl.ds(pl.multiple_of(zh * 8, 8), 8)
    table[me, rows, :] = gains

    sent = []
    arrive = {}
    for dy in (0, 4, 3, 5, 2, 6, 1, 7):
        for dz in (2, 1, 3, 0):
            if dy or dz:
                copy = remote(table.at[me, rows], table.at[me, rows], g_send.at[dy, dz], g_recv.at[dy, dz], at(dz, 0, dy))
                copy.start()
                sent.append(copy)
                arrive[dy, dz] = copy
    last = []
    for dy in (0, 1, 7, 2, 6, 3, 5, 4):
        for dz in range(NZ):
            if dy or dz:
                arrive[dy, dz].wait_recv()
        here = feature_at(NY - dy)
        for dx in (2, 1, 3):
            copy = remote(table.at[here], table.at[here], x_send.at[dx, dy], x_recv.at[dx, dy], at(0, dx, 0))
            copy.start()
            sent.append(copy)
            last.append(copy)

    top = jnp.max(table[pl.ds(x * 8, 8)], axis=0)
    over = jnp.broadcast_to(jnp.max(top, axis=1, keepdims=True), (NODES, HALF))
    lane = lax.broadcasted_iota(jnp.int32, (NODES, HALF), 1)
    node = lax.broadcasted_iota(jnp.int32, (NODES, HALF), 0)
    over = jnp.max(jnp.where(lane == node, over, -jnp.inf), axis=0, keepdims=True)
    tops[0] = jnp.broadcast_to(over, (8, HALF))
    fins = []
    for n in range(1, 16):
        copy = remote(tops.at[0], tops.at[n], f_send.at[n], f_recv.at[n], at(0, n // 4, 0, (n // 2) % 2, n % 2))
        copy.start()
        fins.append(copy)

    for a, b in others:
        remote(acc.at[0, pl.ds(0, QUARTER)], inbox.at[a, b], h_send.at[a, b], h_recv.at[a, b], at(b, 0, 2 * a)).wait_send()
    for copy in last:
        copy.wait_recv()
    for copy in fins:
        copy.wait_recv()
    best[...] = jnp.max(tops[...], axis=0)[:1]
    for copy in sent + fins:
        copy.wait_send()


def per_device(bin_ids, node_ids, gradients, hessians):
    f32 = jnp.float32
    aux = jnp.stack([node_ids.astype(f32), gradients.astype(f32), hessians.astype(f32)]).reshape(3, ROWS // HALF, HALF)
    dma = pltpu.SemaphoreType.DMA
    table, best = pl.pallas_call(
        kernel,
        out_shape=(
            jax.ShapeDtypeStruct((NX * NY, NODES, BINS), f32),
            jax.ShapeDtypeStruct((1, HALF), f32),
        ),
        in_specs=[pl.BlockSpec(memory_space=pl.ANY)] * 2,
        out_specs=(pl.BlockSpec(memory_space=pltpu.VMEM), pl.BlockSpec(memory_space=pltpu.VMEM)),
        scratch_shapes=[
            pltpu.VMEM((8, NG, ROWS), jnp.int32),
            pltpu.VMEM((8, 3, ROWS // HALF, HALF), f32),
            pltpu.VMEM((8, CH, ROWS), jnp.bfloat16),
            pltpu.VMEM((NG, CH, BINS), f32),
            pltpu.VMEM((4, NZ, QUARTER, BINS), f32),
            pltpu.VMEM((16, 8, HALF), f32),
            dma((2,)),
            dma((8,)), dma((8,)),
            dma((8,)), dma((8,)),
            dma((4, NZ)), dma((4, NZ)),
            dma((NY, NZ)), dma((NY, NZ)),
            dma((NX, NY)), dma((NX, NY)),
            dma((16,)), dma((16,)),
            pltpu.SemaphoreType.REGULAR((2,)),
        ],
        compiler_params=pltpu.CompilerParams(collective_id=0, has_side_effects=True, vmem_limit_bytes=40 * 2**20),
        cost_estimate=pl.CostEstimate(flops=2 * 32 * ROWS * CH * BINS, bytes_accessed=2 * 2**20, transcendentals=0),
        name="split_gains",
    )(bin_ids, aux)
    return table, best[0, :NODES]


def solution(mesh):
    in_specs = (P("feat", "rows"), P("rows"), P("rows"), P("rows"))
    out_specs = (P("feat", None, None), P())
    return jax.shard_map(per_device, mesh=mesh, in_specs=in_specs, out_specs=out_specs, check_vma=False)
```

time: 66.1 us -> 57.8 us (0.87)
  Pallas kernels: 62 us -> 53.8 us
    pallas_call x1, Pallas kernels: 62 us -> 53.8 us  [per_device(): pl.pallas_call(kernel, out_shape=(jax.ShapeDtypeStruct((NX * NY, NODES, B...]
where the time goes in v2:
time: 57.8 us; the launch traced here: 57.6 us
  Pallas kernels  53.8 us (93%)
  local copies, waits for them, and re-layouts  2.44 us (4%)
  other arithmetic  0.72 us (1%)
  between operations  0.68 us (1%)
    pallas_call x1, Pallas kernels, per_device(): pl.pallas_call(kernel, out_shape=(jax.ShapeDtypeStruct((NX * NY, NODES, B...  53.8 us
    unnamed x7, local copies, waits for them, and re-layouts  1.92 us

profile of v2, /device:TPU:1, one launch (start us, length us, event | category | flops | bytes accessed | tf_op | source)
XLA Modules:
  0.0 57.6 jit_solution(2662138656229725129)
XLA Ops:
  0.6 0.0 copy-start.1
  0.6 0.0 copy-start.2
  0.7 0.7 %convert_bitcast_fusion = f32[1,16,128]{2,1,0:T(8,128)S(1)} fusion(s32[2048]{0:T(1024)} %param.5), kind=kLoop, calls=%fused_computation.1 | loop fusion | flops 2048 | bytes 16384 | tf_op jit(solution)/shard_map/stack | solution.py:223
  1.4 0.0 copy-done.1
  1.4 0.0 copy-done.2
  1.4 0.0 copy-start
  1.4 0.9 %copy-done = s32[32,2048]{1,0:T(8,128)S(1)} copy-done((s32[32,2048]{1,0:T(8,128)S(1)}, s32[32,2048]{1,0:T(8,128)}, u32[]{:S(2)}) %copy-start) | copy-done | bytes 262168
  2.3 53.8 %split_gains.1 = (f32[32,32,256]{2,1,0:T(8,128)S(1)}, f32[1,128]{1,0:T(1,128)S(1)}) custom-call(s32[32,2048]{1,0:T(8,128)S(1)} %copy-done, f32[3,16,128]{2,1,0:T(8,128)S(1)} %pad_maximum_fusion.aux_hbm), custom_call_target="tpu_custom_call" | custom-call | flops 2147483648 | bytes 2097152 | tf_op jit(solution)/shard_map/split_gains/pallas_call | solution.py:225
  56.1 0.5 slice_bitcast_fusion
  56.6 1.0 %copy.7 = f32[32,32,256]{2,1,0:T(8,128)} copy(f32[32,32,256]{2,1,0:T(8,128)S(1)} %get-tuple-element.10) | data formatting | bytes 2097152
  (2 shorter events, 0.0 us)
Async XLA Ops:
  0.6 0.7 %copy-start.1 = (bf16[2048]{0:T(1024)(128)(2,1)S(1)}, bf16[2048]{0:T(1024)(128)(2,1)}, u32[]{:S(2)}) copy-start(bf16[2048]{0:T(1024)(128)(2,1)} %param.7) | copy-start | bytes 12292
  0.6 0.7 %copy-start.2 = (bf16[2048]{0:T(1024)(128)(2,1)S(1)}, bf16[2048]{0:T(1024)(128)(2,1)}, u32[]{:S(2)}) copy-start(bf16[2048]{0:T(1024)(128)(2,1)} %param.6) | copy-start | bytes 12292
  1.4 1.0 %copy-start = (s32[32,2048]{1,0:T(8,128)S(1)}, s32[32,2048]{1,0:T(8,128)}, u32[]{:S(2)}) copy-start(s32[32,2048]{1,0:T(8,128)} %bins_hbm.1) | copy-start | bytes 786436

commit v3 on v2

--- a/solution.py
+++ b/solution.py
@@ -62,9 +62,9 @@
 
 
 def kernel(bins_hbm, aux_hbm, table, best,
-           bins, aux, weights, acc, inbox, tops,
+           bins, aux, weights, acc, inbox, tops, tops_z, tops_y,
            local_sems, a_send, a_recv, w_send, w_recv, h_send, h_recv,
-           g_send, g_recv, x_send, x_recv, f_send, f_recv, ready):
+           g_send, g_recv, x_send, x_recv, f_send, f_recv, fz_send, fz_recv, fy_send, fy_recv, ready):
     r = lax.axis_index("rows")
     f = lax.axis_index("feat")
     zh, x, y = r // (NX * NY), (r // NY) % NX, r % NY
@@ -124,7 +124,7 @@
     for d in (2, 1, 3):
         pl.semaphore_signal(ready.at[1], inc=1, device_id=at(d, 0, 0), device_id_type=MESH)
 
-    for s in (2, 6, 1):
+    for s in (2, 6, 1, 4, 3, 7):
         for copy in exchange[s]:
             copy.wait()
         build_weights(aux, weights, s)
@@ -133,21 +133,17 @@
         def _(j):
             acc[j] = acc[j] + side_by_side(partial_hist(bins, weights, levels, s, j))
 
-    for s in (4, 3, 7, 5):
-        for copy in exchange[s]:
-            copy.wait()
-        build_weights(aux, weights, s)
+    for copy in exchange[5]:
+        copy.wait()
+    build_weights(aux, weights, 5)
     pl.semaphore_wait(ready.at[1], 3)
 
-    @pl.loop(0, NG, unroll=2)
+    @pl.loop(0, NG, unroll=4)
     def _(i):
         m = (i + 1) // 2
         a = (2 + m * (1 - 2 * (i % 2))) % 4
         j = (yh + a) % 4
-        d = partial_hist(bins, weights, levels, 4, j)
-        for s in (3, 7, 5):
-            d += partial_hist(bins, weights, levels, s, j)
-        acc[j] = acc[j] + side_by_side(d)
+        acc[j] = acc[j] + side_by_side(partial_hist(bins, weights, levels, 5, j))
         for b in (2, 1, 3, 0):
             quarter = pl.ds(pl.multiple_of(((zh + b) % NZ) * QUARTER, QUARTER), QUARTER)
 
@@ -174,47 +170,62 @@
     rows = pl.ds(pl.multiple_of(zh * 8, 8), 8)
     table[me, rows, :] = gains
 
+    def gain_rows(dy, dz):
+        return table.at[feature_at(NY - dy), pl.ds(pl.multiple_of(((zh + NZ - dz) % NZ) * 8, 8), 8)]
+
+    offsets = sorted(((dy, dz) for dy in range(NY) for dz in range(NZ)), key=lambda o: min(o[0], NY - o[0]) + 2 * min(o[1], NZ - o[1]))
     sent = []
     arrive = {}
-    for dy in (0, 4, 3, 5, 2, 6, 1, 7):
-        for dz in (2, 1, 3, 0):
-            if dy or dz:
-                copy = remote(table.at[me, rows], table.at[me, rows], g_send.at[dy, dz], g_recv.at[dy, dz], at(dz, 0, dy))
-                copy.start()
-                sent.append(copy)
-                arrive[dy, dz] = copy
     last = []
-    for dy in (0, 1, 7, 2, 6, 3, 5, 4):
-        for dz in range(NZ):
-            if dy or dz:
-                arrive[dy, dz].wait_recv()
-        here = feature_at(NY - dy)
-        for dx in (2, 1, 3):
-            copy = remote(table.at[here], table.at[here], x_send.at[dx, dy], x_recv.at[dx, dy], at(0, dx, 0))
+
+    def forward(dy, dz):
+        for dx in (1, 3, 2):
+            copy = remote(gain_rows(dy, dz), gain_rows(dy, dz), x_send.at[dx, dy, dz], x_recv.at[dx, dy, dz], at(0, dx, 0))
             copy.start()
             sent.append(copy)
             last.append(copy)
 
-    top = jnp.max(table[pl.ds(x * 8, 8)], axis=0)
-    over = jnp.broadcast_to(jnp.max(top, axis=1, keepdims=True), (NODES, HALF))
-    lane = lax.broadcasted_iota(jnp.int32, (NODES, HALF), 1)
-    node = lax.broadcasted_iota(jnp.int32, (NODES, HALF), 0)
-    over = jnp.max(jnp.where(lane == node, over, -jnp.inf), axis=0, keepdims=True)
-    tops[0] = jnp.broadcast_to(over, (8, HALF))
-    fins = []
-    for n in range(1, 16):
-        copy = remote(tops.at[0], tops.at[n], f_send.at[n], f_recv.at[n], at(0, n // 4, 0, (n // 2) % 2, n % 2))
+    for dy, dz in offsets[1:]:
+        copy = remote(gain_rows(0, 0), gain_rows(0, 0), g_send.at[dy, dz], g_recv.at[dy, dz], at(dz, 0, dy))
         copy.start()
-        fins.append(copy)
+        sent.append(copy)
+        arrive[dy, dz] = copy
+
+    lane = lax.broadcasted_iota(jnp.int32, (8, HALF), 1)
+    node = lax.broadcasted_iota(jnp.int32, (8, HALF), 0) + zh * 8
+    top = jnp.broadcast_to(jnp.max(gains, axis=1, keepdims=True), (8, HALF))
+    top = jnp.max(jnp.where(lane == node, top, -jnp.inf), axis=0, keepdims=True)
+
+    def share(top, slots, send, recv, partners):
+        slots[0] = jnp.broadcast_to(top, (8, HALF))
+        copies = []
+        for n, to in enumerate(partners, 1):
+            copies.append(remote(slots.at[0], slots.at[n], send.at[n], recv.at[n], to))
+            copies[-1].start()
+        sent.extend(copies)
+        return copies
+
+    def gather_top(slots, copies):
+        for copy in copies:
+            copy.wait_recv()
+        return jnp.max(slots[...], axis=0)[:1]
+
+    shared = share(top, tops, f_send, f_recv, [at(0, n // 4, 0, (n // 2) % 2, n % 2) for n in range(1, 16)])
+    forward(0, 0)
+    for n, (dy, dz) in enumerate(offsets[1:]):
+        arrive[dy, dz].wait_recv()
+        forward(dy, dz)
+        if n == 9:
+            shared = share(gather_top(tops, shared), tops_z, fz_send, fz_recv, [at(d, 0, 0) for d in (1, 3, 2)])
+        if n == 21:
+            shared = share(gather_top(tops_z, shared), tops_y, fy_send, fy_recv, [at(0, 0, d) for d in (4, 3, 5, 2, 6, 1, 7)])
 
     for a, b in others:
         remote(acc.at[0, pl.ds(0, QUARTER)], inbox.at[a, b], h_send.at[a, b], h_recv.at[a, b], at(b, 0, 2 * a)).wait_send()
     for copy in last:
         copy.wait_recv()
-    for copy in fins:
-        copy.wait_recv()
-    best[...] = jnp.max(tops[...], axis=0)[:1]
-    for copy in sent + fins:
+    best[...] = gather_top(tops_y, shared)
+    for copy in sent:
         copy.wait_send()
 
 
@@ -237,13 +248,17 @@
             pltpu.VMEM((NG, CH, BINS), f32),
             pltpu.VMEM((4, NZ, QUARTER, BINS), f32),
             pltpu.VMEM((16, 8, HALF), f32),
+            pltpu.VMEM((NZ, 8, HALF), f32),
+            pltpu.VMEM((NY, 8, HALF), f32),
             dma((2,)),
             dma((8,)), dma((8,)),
             dma((8,)), dma((8,)),
             dma((4, NZ)), dma((4, NZ)),
             dma((NY, NZ)), dma((NY, NZ)),
-            dma((NX, NY)), dma((NX, NY)),
+            dma((NX, NY, NZ)), dma((NX, NY, NZ)),
             dma((16,)), dma((16,)),
+            dma((NZ,)), dma((NZ,)),
+            dma((NY,)), dma((NY,)),
             pltpu.SemaphoreType.REGULAR((2,)),
         ],
         compiler_params=pltpu.CompilerParams(collective_id=0, has_side_effects=True, vmem_limit_bytes=40 * 2**20),

time: 57.8 us -> 55.4 us (0.958); the launches traced: 57.6 us -> 54.5 us
  Pallas kernels: 53.8 us -> 50.7 us
    pallas_call x1, Pallas kernels: 53.8 us -> 50.7 us  [per_device(): pl.pallas_call(kernel, out_shape=(jax.ShapeDtypeStruct((NX * NY, NODES, B...]
where the time goes in v3:
time: 55.4 us; the launch traced here: 54.5 us
  Pallas kernels  50.7 us (92%)
  local copies, waits for them, and re-layouts  2.44 us (4%)
  other arithmetic  0.72 us (1%)
  between operations  0.68 us (1%)
    pallas_call x1, Pallas kernels, per_device(): pl.pallas_call(kernel, out_shape=(jax.ShapeDtypeStruct((NX * NY, NODES, B...  50.7 us
    unnamed x7, local copies, waits for them, and re-layouts  1.92 us

profile of v3, /device:TPU:1, one launch (start us, length us, event | category | flops | bytes accessed | tf_op | source)
XLA Modules:
  0.0 54.5 jit_solution(4083786907066153196)
XLA Ops:
  0.6 0.0 copy-start.1
  0.6 0.0 copy-start.2
  0.7 0.7 %convert_bitcast_fusion = f32[1,16,128]{2,1,0:T(8,128)S(1)} fusion(s32[2048]{0:T(1024)} %param.5), kind=kLoop, calls=%fused_computation.1 | loop fusion | flops 2048 | bytes 16384 | tf_op jit(solution)/shard_map/stack | solution.py:234
  1.4 0.0 copy-done.1
  1.4 0.0 copy-done.2
  1.4 0.0 copy-start
  1.4 0.9 %copy-done = s32[32,2048]{1,0:T(8,128)S(1)} copy-done((s32[32,2048]{1,0:T(8,128)S(1)}, s32[32,2048]{1,0:T(8,128)}, u32[]{:S(2)}) %copy-start) | copy-done | bytes 262168
  2.3 50.7 %split_gains.1 = (f32[32,32,256]{2,1,0:T(8,128)S(1)}, f32[1,128]{1,0:T(1,128)S(1)}) custom-call(s32[32,2048]{1,0:T(8,128)S(1)} %copy-done, f32[3,16,128]{2,1,0:T(8,128)S(1)} %pad_maximum_fusion.aux_hbm), custom_call_target="tpu_custom_call" | custom-call | flops 2147483648 | bytes 2097152 | tf_op jit(solution)/shard_map/split_gains/pallas_call | solution.py:236
  53.1 0.5 slice_bitcast_fusion
  53.6 1.0 %copy.7 = f32[32,32,256]{2,1,0:T(8,128)} copy(f32[32,32,256]{2,1,0:T(8,128)S(1)} %get-tuple-element.10) | data formatting | bytes 2097152
  (2 shorter events, 0.0 us)
Async XLA Ops:
  0.6 0.7 %copy-start.1 = (bf16[2048]{0:T(1024)(128)(2,1)S(1)}, bf16[2048]{0:T(1024)(128)(2,1)}, u32[]{:S(2)}) copy-start(bf16[2048]{0:T(1024)(128)(2,1)} %param.7) | copy-start | bytes 12292
  0.6 0.7 %copy-start.2 = (bf16[2048]{0:T(1024)(128)(2,1)S(1)}, bf16[2048]{0:T(1024)(128)(2,1)}, u32[]{:S(2)}) copy-start(bf16[2048]{0:T(1024)(128)(2,1)} %param.6) | copy-start | bytes 12292
  1.4 1.0 %copy-start = (s32[32,2048]{1,0:T(8,128)S(1)}, s32[32,2048]{1,0:T(8,128)}, u32[]{:S(2)}) copy-start(s32[32,2048]{1,0:T(8,128)} %bins_hbm.1) | copy-start | bytes 786436

commit v4 on v3

--- a/solution.py
+++ b/solution.py
@@ -64,7 +64,7 @@
 def kernel(bins_hbm, aux_hbm, table, best,
            bins, aux, weights, acc, inbox, tops, tops_z, tops_y,
            local_sems, a_send, a_recv, w_send, w_recv, h_send, h_recv,
-           g_send, g_recv, x_send, x_recv, f_send, f_recv, fz_send, fz_recv, fy_send, fy_recv, ready):
+           g_send, g_recv, x_send, x_recv, f_send, f_recv, ready):
     r = lax.axis_index("rows")
     f = lax.axis_index("feat")
     zh, x, y = r // (NX * NY), (r // NY) % NX, r % NY
@@ -103,8 +103,8 @@
         s = dx * 2 + p
         to = pair(dx, p)
         exchange[s] = (
-            remote(aux_hbm, aux.at[s], w_send.at[s], w_recv.at[s], to),
-            remote(bins_hbm.at[features_of(dx, p)], bins.at[s], a_send.at[s], a_recv.at[s], to),
+            remote(aux_hbm, aux.at[s], w_send.at[0], w_recv.at[s], to),
+            remote(bins_hbm.at[features_of(dx, p)], bins.at[s], a_send.at[0], a_recv.at[s], to),
         )
         for copy in exchange[s]:
             copy.start()
@@ -126,7 +126,7 @@
 
     for s in (2, 6, 1, 4, 3, 7):
         for copy in exchange[s]:
-            copy.wait()
+            copy.wait_recv()
         build_weights(aux, weights, s)
 
         @pl.loop(0, NG, unroll=4)
@@ -134,7 +134,7 @@
             acc[j] = acc[j] + side_by_side(partial_hist(bins, weights, levels, s, j))
 
     for copy in exchange[5]:
-        copy.wait()
+        copy.wait_recv()
     build_weights(aux, weights, 5)
     pl.semaphore_wait(ready.at[1], 3)
 
@@ -149,13 +149,17 @@
 
             @pl.when(a + b > 0)
             def _():
-                remote(acc.at[j, quarter], inbox.at[a, b], h_send.at[a, b], h_recv.at[a, b], at(b, 0, 2 * a)).start()
+                remote(acc.at[j, quarter], inbox.at[a, b], h_send.at[(a + 3) // 4], h_recv.at[(a + 3) // 4], at(b, 0, 2 * a)).start()
 
     hist = acc[yh, pl.ds(pl.multiple_of(zh * QUARTER, QUARTER), QUARTER), :]
-    others = [(a, b) for a in (0, 1, 3, 2) for b in (0, 1, 3, 2) if a or b]
-    for a, b in others:
-        remote(acc.at[0, pl.ds(0, QUARTER)], inbox.at[a, b], h_send.at[a, b], h_recv.at[a, b], at(b, 0, 2 * a)).wait_recv()
-        hist = hist + inbox[a, b]
+    nearby = remote(inbox.at[0, pl.ds(1, 3)], inbox.at[0, pl.ds(1, 3)], h_send.at[0], h_recv.at[0], at(1, 0, 0))
+    beyond = remote(inbox.at[pl.ds(1, 3)], inbox.at[pl.ds(1, 3)], h_send.at[1], h_recv.at[1], at(1, 0, 0))
+    nearby.wait_recv()
+    for b in range(1, 4):
+        hist = hist + inbox[0, b]
+    beyond.wait_recv()
+    for a in range(1, 4):
+        hist = hist + ((inbox[a, 0] + inbox[a, 1]) + (inbox[a, 2] + inbox[a, 3]))
 
     left, whole = prefix_sums(hist)
     lg, lh, tg, th = left[:8], left[8:], whole[:8], whole[8:]
@@ -174,59 +178,60 @@
         return table.at[feature_at(NY - dy), pl.ds(pl.multiple_of(((zh + NZ - dz) % NZ) * 8, 8), 8)]
 
     offsets = sorted(((dy, dz) for dy in range(NY) for dz in range(NZ)), key=lambda o: min(o[0], NY - o[0]) + 2 * min(o[1], NZ - o[1]))
-    sent = []
     arrive = {}
-    last = []
 
     def forward(dy, dz):
         for dx in (1, 3, 2):
-            copy = remote(gain_rows(dy, dz), gain_rows(dy, dz), x_send.at[dx, dy, dz], x_recv.at[dx, dy, dz], at(0, dx, 0))
-            copy.start()
-            sent.append(copy)
-            last.append(copy)
+            remote(gain_rows(dy, dz), gain_rows(dy, dz), x_send, x_recv, at(0, dx, 0)).start()
 
     for dy, dz in offsets[1:]:
-        copy = remote(gain_rows(0, 0), gain_rows(0, 0), g_send.at[dy, dz], g_recv.at[dy, dz], at(dz, 0, dy))
-        copy.start()
-        sent.append(copy)
-        arrive[dy, dz] = copy
+        arrive[dy, dz] = remote(gain_rows(0, 0), gain_rows(0, 0), g_send.at[min(dy, 1)], g_recv.at[dy, dz], at(dz, 0, dy))
+        arrive[dy, dz].start()
 
     lane = lax.broadcasted_iota(jnp.int32, (8, HALF), 1)
     node = lax.broadcasted_iota(jnp.int32, (8, HALF), 0) + zh * 8
     top = jnp.broadcast_to(jnp.max(gains, axis=1, keepdims=True), (8, HALF))
     top = jnp.max(jnp.where(lane == node, top, -jnp.inf), axis=0, keepdims=True)
 
-    def share(top, slots, send, recv, partners):
+    def share(top, slots, n, partners):
         slots[0] = jnp.broadcast_to(top, (8, HALF))
-        copies = []
-        for n, to in enumerate(partners, 1):
-            copies.append(remote(slots.at[0], slots.at[n], send.at[n], recv.at[n], to))
-            copies[-1].start()
-        sent.extend(copies)
-        return copies
-
-    def gather_top(slots, copies):
-        for copy in copies:
-            copy.wait_recv()
+        for m, to in enumerate(partners, 1):
+            remote(slots.at[0], slots.at[m], f_send.at[n], f_recv.at[n], to).start()
+
+    def shared(slots, n):
+        others = slots.at[pl.ds(1, slots.shape[0] - 1)]
+        return remote(others, others, f_send.at[n], f_recv.at[n], at(1, 0, 0))
+
+    def gather_top(slots, n):
+        shared(slots, n).wait_recv()
         return jnp.max(slots[...], axis=0)[:1]
 
-    shared = share(top, tops, f_send, f_recv, [at(0, n // 4, 0, (n // 2) % 2, n % 2) for n in range(1, 16)])
+    share(top, tops, 0, [at(0, n // 4, 0, (n // 2) % 2, n % 2) for n in range(1, 16)])
     forward(0, 0)
     for n, (dy, dz) in enumerate(offsets[1:]):
         arrive[dy, dz].wait_recv()
         forward(dy, dz)
         if n == 9:
-            shared = share(gather_top(tops, shared), tops_z, fz_send, fz_recv, [at(d, 0, 0) for d in (1, 3, 2)])
+            share(gather_top(tops, 0), tops_z, 1, [at(d, 0, 0) for d in (1, 3, 2)])
         if n == 21:
-            shared = share(gather_top(tops_z, shared), tops_y, fy_send, fy_recv, [at(0, 0, d) for d in (4, 3, 5, 2, 6, 1, 7)])
-
-    for a, b in others:
-        remote(acc.at[0, pl.ds(0, QUARTER)], inbox.at[a, b], h_send.at[a, b], h_recv.at[a, b], at(b, 0, 2 * a)).wait_send()
-    for copy in last:
-        copy.wait_recv()
-    best[...] = gather_top(tops_y, shared)
-    for copy in sent:
-        copy.wait_send()
+            share(gather_top(tops_z, 1), tops_y, 2, [at(0, 0, d) for d in (4, 3, 5, 2, 6, 1, 7)])
+
+    planes = table.at[pl.ds(0, 3 * NY)]
+    passed_on = remote(planes, planes, x_send, x_recv, at(0, 1, 0))
+    passed_on.wait_recv()
+    best[...] = gather_top(tops_y, 2)[:, :NODES]
+
+    passed_on.wait_send()
+    along_z = table.at[0, pl.ds(0, 8 * (NZ - 1))]
+    along_y = table.at[pl.ds(0, NY - 1)]
+    remote(along_z, along_z, g_send.at[0], x_recv, at(1, 0, 0)).wait_send()
+    remote(along_y, along_y, g_send.at[1], x_recv, at(0, 0, 1)).wait_send()
+    for n, slots in enumerate((tops, tops_z, tops_y)):
+        shared(slots, n).wait_send()
+    nearby.wait_send()
+    beyond.wait_send()
+    remote(aux.at[pl.ds(1, 7)], aux.at[pl.ds(1, 7)], w_send.at[0], w_recv.at[1], at(1, 0, 0)).wait_send()
+    remote(bins.at[pl.ds(1, 7)], bins.at[pl.ds(1, 7)], a_send.at[0], a_recv.at[1], at(1, 0, 0)).wait_send()
 
 
 def per_device(bin_ids, node_ids, gradients, hessians):
@@ -237,7 +242,7 @@
         kernel,
         out_shape=(
             jax.ShapeDtypeStruct((NX * NY, NODES, BINS), f32),
-            jax.ShapeDtypeStruct((1, HALF), f32),
+            jax.ShapeDtypeStruct((1, NODES), f32),
         ),
         in_specs=[pl.BlockSpec(memory_space=pl.ANY)] * 2,
         out_specs=(pl.BlockSpec(memory_space=pltpu.VMEM), pl.BlockSpec(memory_space=pltpu.VMEM)),
@@ -251,21 +256,19 @@
             pltpu.VMEM((NZ, 8, HALF), f32),
             pltpu.VMEM((NY, 8, HALF), f32),
             dma((2,)),
-            dma((8,)), dma((8,)),
-            dma((8,)), dma((8,)),
-            dma((4, NZ)), dma((4, NZ)),
-            dma((NY, NZ)), dma((NY, NZ)),
-            dma((NX, NY, NZ)), dma((NX, NY, NZ)),
-            dma((16,)), dma((16,)),
-            dma((NZ,)), dma((NZ,)),
-            dma((NY,)), dma((NY,)),
+            dma((1,)), dma((8,)),
+            dma((1,)), dma((8,)),
+            dma((2,)), dma((2,)),
+            dma((2,)), dma((NY, NZ)),
+            dma, dma,
+            dma((3,)), dma((3,)),
             pltpu.SemaphoreType.REGULAR((2,)),
         ],
         compiler_params=pltpu.CompilerParams(collective_id=0, has_side_effects=True, vmem_limit_bytes=40 * 2**20),
         cost_estimate=pl.CostEstimate(flops=2 * 32 * ROWS * CH * BINS, bytes_accessed=2 * 2**20, transcendentals=0),
         name="split_gains",
     )(bin_ids, aux)
-    return table, best[0, :NODES]
+    return table, best.reshape(NODES)
 
 
 def solution(mesh):

time: 55.4 us -> 51.7 us (0.933)
  Pallas kernels: 50.7 us -> 47.4 us
    pallas_call x1, Pallas kernels: 50.7 us -> 47.4 us  [per_device(): pl.pallas_call(kernel, out_shape=(jax.ShapeDtypeStruct((NX * NY, NODES, B...]
    unnamed x7 -> x8, local copies, waits for them, and re-layouts: 1.92 us -> 2.44 us
where the time goes in v4:
time: 51.7 us; the launch traced here: 51.2 us
  Pallas kernels  47.4 us (92%)
  local copies, waits for them, and re-layouts  2.44 us (5%)
  other arithmetic  0.72 us (1%)
  between operations  0.68 us (1%)
    pallas_call x1, Pallas kernels, per_device(): pl.pallas_call(kernel, out_shape=(jax.ShapeDtypeStruct((NX * NY, NODES, B...  47.4 us
    unnamed x8, local copies, waits for them, and re-layouts  2.44 us

profile of v4, /device:TPU:1, one launch (start us, length us, event | category | flops | bytes accessed | tf_op | source)
XLA Modules:
  0.0 51.2 jit_solution(17710887123324225399)
XLA Ops:
  0.6 0.0 copy-start.1
  0.6 0.0 copy-start.2
  0.7 0.7 %convert_bitcast_fusion = f32[1,16,128]{2,1,0:T(8,128)S(1)} fusion(s32[2048]{0:T(1024)} %param.5), kind=kLoop, calls=%fused_computation.1 | loop fusion | flops 2048 | bytes 16384 | tf_op jit(solution)/shard_map/stack | solution.py:239
  1.4 0.0 copy-done.1
  1.4 0.0 copy-done.2
  1.4 0.0 copy-start
  1.4 0.9 %copy-done = s32[32,2048]{1,0:T(8,128)S(1)} copy-done((s32[32,2048]{1,0:T(8,128)S(1)}, s32[32,2048]{1,0:T(8,128)}, u32[]{:S(2)}) %copy-start) | copy-done | bytes 262168
  2.3 47.4 %split_gains.1 = (f32[32,32,256]{2,1,0:T(8,128)S(1)}, f32[1,32]{1,0:T(1,128)S(1)}) custom-call(s32[32,2048]{1,0:T(8,128)S(1)} %copy-done, f32[3,16,128]{2,1,0:T(8,128)S(1)} %pad_maximum_fusion.aux_hbm), custom_call_target="tpu_custom_call" | custom-call | flops 2147483648 | bytes 2097152 | tf_op jit(solution)/shard_map/split_gains/pallas_call | solution.py:241
  49.7 1.0 %copy.8 = f32[32,32,256]{2,1,0:T(8,128)} copy(f32[32,32,256]{2,1,0:T(8,128)S(1)} %get-tuple-element.10) | data formatting | bytes 2097152
  50.7 0.5 copy.9
  (2 shorter events, 0.0 us)
Async XLA Ops:
  0.6 0.7 %copy-start.1 = (bf16[2048]{0:T(1024)(128)(2,1)S(1)}, bf16[2048]{0:T(1024)(128)(2,1)}, u32[]{:S(2)}) copy-start(bf16[2048]{0:T(1024)(128)(2,1)} %param.7) | copy-start | bytes 12292
  0.6 0.7 %copy-start.2 = (bf16[2048]{0:T(1024)(128)(2,1)S(1)}, bf16[2048]{0:T(1024)(128)(2,1)}, u32[]{:S(2)}) copy-start(bf16[2048]{0:T(1024)(128)(2,1)} %param.6) | copy-start | bytes 12292
  1.4 1.0 %copy-start = (s32[32,2048]{1,0:T(8,128)S(1)}, s32[32,2048]{1,0:T(8,128)}, u32[]{:S(2)}) copy-start(s32[32,2048]{1,0:T(8,128)} %bins_hbm.1) | copy-start | bytes 786436

commit v5 on v4

--- a/solution.py
+++ b/solution.py
@@ -64,19 +64,23 @@
 def kernel(bins_hbm, aux_hbm, table, best,
            bins, aux, weights, acc, inbox, tops, tops_z, tops_y,
            local_sems, a_send, a_recv, w_send, w_recv, h_send, h_recv,
-           g_send, g_recv, x_send, x_recv, f_send, f_recv, ready):
+           g_send, g_recv, x_send, x_recv, f_send, f_recv, c_send, c_recv, ready):
     r = lax.axis_index("rows")
     f = lax.axis_index("feat")
-    zh, x, y = r // (NX * NY), (r // NY) % NX, r % NY
-    zl, core = f // 2, f % 2
-    yh, yl = y // 2, y % 2
+    zh, x, y = lax.div(r, NX * NY), lax.rem(lax.div(r, NY), NX), lax.rem(r, NY)
+    zl, core = lax.div(f, 2), lax.rem(f, 2)
+    yh, yl = lax.div(y, 2), lax.rem(y, 2)
+    at_x = [lax.rem(x + d, NX) for d in range(NX)]
+    at_y = [lax.rem(y + d, NY) for d in range(NY)]
+    at_z = [lax.rem(zh + d, NZ) for d in range(NZ)]
 
     def at(dz, dx, dy, dzl=0, dc=0):
-        row = (((zh + dz) % NZ) * NX + (x + dx) % NX) * NY + (y + dy) % NY
-        return (row, ((zl + dzl) % 2) * 2 + (core + dc) % 2)
+        there = at_y[dy] if isinstance(dy, int) else lax.rem(y + dy, NY)
+        row = (at_z[dz] * NX + at_x[dx]) * NY + there
+        return (row, (zl * (1 - dzl) + (1 - zl) * dzl) * 2 + core * (1 - dc) + (1 - core) * dc)
 
     def pair(dx, p):
-        return at(0, dx, (1 - 2 * yl) * p)
+        return at(0, dx, (NY + 1 - 2 * yl) * p if p else 0)
 
     def remote(src, dst, send, recv, to):
         return pltpu.make_async_remote_copy(src_ref=src, dst_ref=dst, send_sem=send, recv_sem=recv, device_id=to, device_id_type=MESH)
@@ -89,7 +93,7 @@
         pl.semaphore_signal(barrier, inc=1, device_id=to, device_id_type=MESH)
 
     def features_of(dx, p):
-        group = ((x + dx) % NX) * 2 + (yl + p) % 2
+        group = at_x[dx] * 2 + (yl * (1 - p) + (1 - yl) * p)
         return pl.ds(group * NG, NG)
 
     own_bins = pltpu.make_async_copy(bins_hbm.at[features_of(0, 0)], bins.at[0], local_sems.at[0])
@@ -142,10 +146,10 @@
     def _(i):
         m = (i + 1) // 2
         a = (2 + m * (1 - 2 * (i % 2))) % 4
-        j = (yh + a) % 4
+        j = lax.rem(yh + a, 4)
         acc[j] = acc[j] + side_by_side(partial_hist(bins, weights, levels, 5, j))
         for b in (2, 1, 3, 0):
-            quarter = pl.ds(pl.multiple_of(((zh + b) % NZ) * QUARTER, QUARTER), QUARTER)
+            quarter = pl.ds(pl.multiple_of(at_z[b] * QUARTER, QUARTER), QUARTER)
 
             @pl.when(a + b > 0)
             def _():
@@ -167,22 +171,29 @@
     gains = lg * lg / (lh + 1.0) + rg * rg / (rh + 1.0) - tg * tg / (th + 1.0)
 
     def feature_at(dy):
-        there = (y + dy) % NY
-        return (x * 2 + there % 2) * NG + there // 2
+        there = at_y[dy % NY]
+        return (x * 2 + lax.rem(there, 2)) * NG + lax.div(there, 2)
 
     me = feature_at(0)
     rows = pl.ds(pl.multiple_of(zh * 8, 8), 8)
     table[me, rows, :] = gains
 
     def gain_rows(dy, dz):
-        return table.at[feature_at(NY - dy), pl.ds(pl.multiple_of(((zh + NZ - dz) % NZ) * 8, 8), 8)]
+        return table.at[feature_at(NY - dy), pl.ds(pl.multiple_of(at_z[(NZ - dz) % NZ] * 8, 8), 8)]
 
     offsets = sorted(((dy, dz) for dy in range(NY) for dz in range(NZ)), key=lambda o: min(o[0], NY - o[0]) + 2 * min(o[1], NZ - o[1]))
     arrive = {}
 
     def forward(dy, dz):
-        for dx in (1, 3, 2):
+        for dx in (1, 3):
             remote(gain_rows(dy, dz), gain_rows(dy, dz), x_send, x_recv, at(0, dx, 0)).start()
+        first = gain_rows(dy, dz).at[:, pl.ds(0, HALF)]
+        remote(first, first, x_send, x_recv, at(0, 2, 0)).start()
+
+    second = table.at[me, rows, pl.ds(HALF, HALF)]
+    opposite = table.at[(at_x[2] * 2 + yl) * NG + yh, rows, pl.ds(HALF, HALF)]
+    across = remote(second, second, c_send.at[0], c_recv.at[0], at(0, 2, 0))
+    across.start()
 
     for dy, dz in offsets[1:]:
         arrive[dy, dz] = remote(gain_rows(0, 0), gain_rows(0, 0), g_send.at[min(dy, 1)], g_recv.at[dy, dz], at(dz, 0, dy))
@@ -211,17 +222,26 @@
     for n, (dy, dz) in enumerate(offsets[1:]):
         arrive[dy, dz].wait_recv()
         forward(dy, dz)
-        if n == 9:
+        if n == 10:
+            across.wait_recv()
+            for to_y, to_z in offsets[1:]:
+                remote(opposite, opposite, c_send.at[1], c_recv.at[1], at(to_z, 0, to_y)).start()
+        if n == 15:
             share(gather_top(tops, 0), tops_z, 1, [at(d, 0, 0) for d in (1, 3, 2)])
-        if n == 21:
+        if n == 27:
             share(gather_top(tops_z, 1), tops_y, 2, [at(0, 0, d) for d in (4, 3, 5, 2, 6, 1, 7)])
 
-    planes = table.at[pl.ds(0, 3 * NY)]
+    planes = table.at[pl.ds(0, 5 * NY // 2)]
     passed_on = remote(planes, planes, x_send, x_recv, at(0, 1, 0))
     passed_on.wait_recv()
+    spread = table.at[pl.ds(0, NY * NZ - 1), pl.ds(0, 8), pl.ds(0, HALF)]
+    seconds = remote(spread, spread, c_send.at[1], c_recv.at[1], at(0, 0, 1))
+    seconds.wait_recv()
     best[...] = gather_top(tops_y, 2)[:, :NODES]
 
     passed_on.wait_send()
+    across.wait_send()
+    seconds.wait_send()
     along_z = table.at[0, pl.ds(0, 8 * (NZ - 1))]
     along_y = table.at[pl.ds(0, NY - 1)]
     remote(along_z, along_z, g_send.at[0], x_recv, at(1, 0, 0)).wait_send()
@@ -262,6 +282,7 @@
             dma((2,)), dma((NY, NZ)),
             dma, dma,
             dma((3,)), dma((3,)),
+            dma((2,)), dma((2,)),
             pltpu.SemaphoreType.REGULAR((2,)),
         ],
         compiler_params=pltpu.CompilerParams(collective_id=0, has_side_effects=True, vmem_limit_bytes=40 * 2**20),

time: 51.7 us -> 52.8 us (1.021)
  the two profiles are of different devices: /device:TPU:1 before, /device:TPU:8 now
where the time goes in v5:
time: 52.8 us; the launch traced here: 52.6 us
  Pallas kernels  48.8 us (92%)
  local copies, waits for them, and re-layouts  2.44 us (5%)
  other arithmetic  0.72 us (1%)
  between operations  0.68 us (1%)
    pallas_call x1, Pallas kernels, per_device(): pl.pallas_call(kernel, out_shape=(jax.ShapeDtypeStruct((NX * NY, NODES, B...  48.8 us
    unnamed x8, local copies, waits for them, and re-layouts  2.44 us

profile of v5, /device:TPU:8, one launch (start us, length us, event | category | flops | bytes accessed | tf_op | source)
XLA Modules:
  0.0 52.6 jit_solution(15065299965279005249)
XLA Ops:
  0.6 0.0 copy-start.1
  0.6 0.0 copy-start.2
  0.7 0.7 %convert_bitcast_fusion = f32[1,16,128]{2,1,0:T(8,128)S(1)} fusion(s32[2048]{0:T(1024)} %param.5), kind=kLoop, calls=%fused_computation.1 | loop fusion | flops 2048 | bytes 16384 | tf_op jit(solution)/shard_map/stack | solution.py:259
  1.4 0.0 copy-done.1
  1.4 0.0 copy-done.2
  1.4 0.0 copy-start
  1.4 0.9 %copy-done = s32[32,2048]{1,0:T(8,128)S(1)} copy-done((s32[32,2048]{1,0:T(8,128)S(1)}, s32[32,2048]{1,0:T(8,128)}, u32[]{:S(2)}) %copy-start) | copy-done | bytes 262168
  2.3 48.8 %split_gains.1 = (f32[32,32,256]{2,1,0:T(8,128)S(1)}, f32[1,32]{1,0:T(1,128)S(1)}) custom-call(s32[32,2048]{1,0:T(8,128)S(1)} %copy-done, f32[3,16,128]{2,1,0:T(8,128)S(1)} %pad_maximum_fusion.aux_hbm), custom_call_target="tpu_custom_call" | custom-call | flops 2147483648 | bytes 2097152 | tf_op jit(solution)/shard_map/split_gains/pallas_call | solution.py:261
  51.1 1.0 %copy.8 = f32[32,32,256]{2,1,0:T(8,128)} copy(f32[32,32,256]{2,1,0:T(8,128)S(1)} %get-tuple-element.10) | data formatting | bytes 2097152
  52.1 0.5 copy.9
  (2 shorter events, 0.0 us)
Async XLA Ops:
  0.6 0.7 %copy-start.1 = (bf16[2048]{0:T(1024)(128)(2,1)S(1)}, bf16[2048]{0:T(1024)(128)(2,1)}, u32[]{:S(2)}) copy-start(bf16[2048]{0:T(1024)(128)(2,1)} %param.7) | copy-start | bytes 12292
  0.6 0.7 %copy-start.2 = (bf16[2048]{0:T(1024)(128)(2,1)S(1)}, bf16[2048]{0:T(1024)(128)(2,1)}, u32[]{:S(2)}) copy-start(bf16[2048]{0:T(1024)(128)(2,1)} %param.6) | copy-start | bytes 12292
  1.4 1.0 %copy-start = (s32[32,2048]{1,0:T(8,128)S(1)}, s32[32,2048]{1,0:T(8,128)}, u32[]{:S(2)}) copy-start(s32[32,2048]{1,0:T(8,128)} %bins_hbm.1) | copy-start | bytes 786436

commit v6 on v5

--- a/solution.py
+++ b/solution.py
@@ -226,9 +226,9 @@
             across.wait_recv()
             for to_y, to_z in offsets[1:]:
                 remote(opposite, opposite, c_send.at[1], c_recv.at[1], at(to_z, 0, to_y)).start()
-        if n == 15:
+        if n == 9:
             share(gather_top(tops, 0), tops_z, 1, [at(d, 0, 0) for d in (1, 3, 2)])
-        if n == 27:
+        if n == 21:
             share(gather_top(tops_z, 1), tops_y, 2, [at(0, 0, d) for d in (4, 3, 5, 2, 6, 1, 7)])
 
     planes = table.at[pl.ds(0, 5 * NY // 2)]

time: 52.8 us -> 50.8 us (0.962)
  the two profiles are of different devices: /device:TPU:8 before, /device:TPU:1 now
where the time goes in v6:
time: 50.8 us; the launch traced here: 50.6 us
  Pallas kernels  46.8 us (92%)
  local copies, waits for them, and re-layouts  2.44 us (5%)
  other arithmetic  0.72 us (1%)
  between operations  0.68 us (1%)
    pallas_call x1, Pallas kernels, per_device(): pl.pallas_call(kernel, out_shape=(jax.ShapeDtypeStruct((NX * NY, NODES, B...  46.8 us
    unnamed x8, local copies, waits for them, and re-layouts  2.44 us

profile of v6, /device:TPU:1, one launch (start us, length us, event | category | flops | bytes accessed | tf_op | source)
XLA Modules:
  0.0 50.6 jit_solution(5190186627582514228)
XLA Ops:
  0.6 0.0 copy-start.1
  0.6 0.0 copy-start.2
  0.7 0.7 %convert_bitcast_fusion = f32[1,16,128]{2,1,0:T(8,128)S(1)} fusion(s32[2048]{0:T(1024)} %param.5), kind=kLoop, calls=%fused_computation.1 | loop fusion | flops 2048 | bytes 16384 | tf_op jit(solution)/shard_map/stack | solution.py:259
  1.4 0.0 copy-done.1
  1.4 0.0 copy-done.2
  1.4 0.0 copy-start
  1.4 0.9 %copy-done = s32[32,2048]{1,0:T(8,128)S(1)} copy-done((s32[32,2048]{1,0:T(8,128)S(1)}, s32[32,2048]{1,0:T(8,128)}, u32[]{:S(2)}) %copy-start) | copy-done | bytes 262168
  2.3 46.8 %split_gains.1 = (f32[32,32,256]{2,1,0:T(8,128)S(1)}, f32[1,32]{1,0:T(1,128)S(1)}) custom-call(s32[32,2048]{1,0:T(8,128)S(1)} %copy-done, f32[3,16,128]{2,1,0:T(8,128)S(1)} %pad_maximum_fusion.aux_hbm), custom_call_target="tpu_custom_call" | custom-call | flops 2147483648 | bytes 2097152 | tf_op jit(solution)/shard_map/split_gains/pallas_call | solution.py:261
  49.1 1.0 %copy.8 = f32[32,32,256]{2,1,0:T(8,128)} copy(f32[32,32,256]{2,1,0:T(8,128)S(1)} %get-tuple-element.10) | data formatting | bytes 2097152
  50.1 0.5 %copy.9 = f32[32]{0:T(128)} copy(f32[32]{0:T(128)S(1)} %bitcast.9) | data formatting | bytes 256
  (2 shorter events, 0.0 us)
Async XLA Ops:
  0.6 0.7 %copy-start.1 = (bf16[2048]{0:T(1024)(128)(2,1)S(1)}, bf16[2048]{0:T(1024)(128)(2,1)}, u32[]{:S(2)}) copy-start(bf16[2048]{0:T(1024)(128)(2,1)} %param.7) | copy-start | bytes 12292
  0.6 0.7 %copy-start.2 = (bf16[2048]{0:T(1024)(128)(2,1)S(1)}, bf16[2048]{0:T(1024)(128)(2,1)}, u32[]{:S(2)}) copy-start(bf16[2048]{0:T(1024)(128)(2,1)} %param.6) | copy-start | bytes 12292
  1.4 1.0 %copy-start = (s32[32,2048]{1,0:T(8,128)S(1)}, s32[32,2048]{1,0:T(8,128)}, u32[]{:S(2)}) copy-start(s32[32,2048]{1,0:T(8,128)} %bins_hbm.1) | copy-start | bytes 786436

commit v7 on v6

--- a/solution.py
+++ b/solution.py
@@ -148,12 +148,10 @@
         a = (2 + m * (1 - 2 * (i % 2))) % 4
         j = lax.rem(yh + a, 4)
         acc[j] = acc[j] + side_by_side(partial_hist(bins, weights, levels, 5, j))
-        for b in (2, 1, 3, 0):
-            quarter = pl.ds(pl.multiple_of(at_z[b] * QUARTER, QUARTER), QUARTER)
-
-            @pl.when(a + b > 0)
-            def _():
-                remote(acc.at[j, quarter], inbox.at[a, b], h_send.at[(a + 3) // 4], h_recv.at[(a + 3) // 4], at(b, 0, 2 * a)).start()
+
+    for a, b in sorted(((a, b) for a in range(4) for b in range(4) if a or b), key=lambda o: min(o[0], 4 - o[0]) + min(o[1], 4 - o[1])):
+        quarter = pl.ds(pl.multiple_of(at_z[b] * QUARTER, QUARTER), QUARTER)
+        remote(acc.at[lax.rem(yh + a, 4), quarter], inbox.at[a, b], h_send.at[min(a, 1)], h_recv.at[min(a, 1)], at(b, 0, 2 * a)).start()
 
     hist = acc[yh, pl.ds(pl.multiple_of(zh * QUARTER, QUARTER), QUARTER), :]
     nearby = remote(inbox.at[0, pl.ds(1, 3)], inbox.at[0, pl.ds(1, 3)], h_send.at[0], h_recv.at[0], at(1, 0, 0))

time: 50.8 us -> 53.8 us (1.059)
  Pallas kernels: 46.8 us -> 49.7 us
    pallas_call x1, Pallas kernels: 46.8 us -> 49.7 us  [per_device(): pl.pallas_call(kernel, out_shape=(jax.ShapeDtypeStruct((NX * NY, NODES, B...]
where the time goes in v7:
time: 53.8 us; the launch traced here: 53.5 us
  Pallas kernels  49.7 us (92%)
  local copies, waits for them, and re-layouts  2.44 us (5%)
  other arithmetic  0.72 us (1%)
  between operations  0.68 us (1%)
    pallas_call x1, Pallas kernels, per_device(): pl.pallas_call(kernel, out_shape=(jax.ShapeDtypeStruct((NX * NY, NODES, B...  49.7 us
    unnamed x8, local copies, waits for them, and re-layouts  2.44 us

profile of v7, /device:TPU:1, one launch (start us, length us, event | category | flops | bytes accessed | tf_op | source)
XLA Modules:
  0.0 53.5 jit_solution(12879751322681476162)
XLA Ops:
  0.6 0.0 copy-start.1
  0.6 0.0 copy-start.2
  0.7 0.7 %convert_bitcast_fusion = f32[1,16,128]{2,1,0:T(8,128)S(1)} fusion(s32[2048]{0:T(1024)} %param.5), kind=kLoop, calls=%fused_computation.1 | loop fusion | flops 2048 | bytes 16384 | tf_op jit(solution)/shard_map/stack | solution.py:257
  1.4 0.0 copy-done.1
  1.4 0.0 copy-done.2
  1.4 0.0 copy-start
  1.4 0.9 %copy-done = s32[32,2048]{1,0:T(8,128)S(1)} copy-done((s32[32,2048]{1,0:T(8,128)S(1)}, s32[32,2048]{1,0:T(8,128)}, u32[]{:S(2)}) %copy-start) | copy-done | bytes 262168
  2.3 49.7 %split_gains.1 = (f32[32,32,256]{2,1,0:T(8,128)S(1)}, f32[1,32]{1,0:T(1,128)S(1)}) custom-call(s32[32,2048]{1,0:T(8,128)S(1)} %copy-done, f32[3,16,128]{2,1,0:T(8,128)S(1)} %pad_maximum_fusion.aux_hbm), custom_call_target="tpu_custom_call" | custom-call | flops 2147483648 | bytes 2097152 | tf_op jit(solution)/shard_map/split_gains/pallas_call | solution.py:259
  52.0 1.0 %copy.8 = f32[32,32,256]{2,1,0:T(8,128)} copy(f32[32,32,256]{2,1,0:T(8,128)S(1)} %get-tuple-element.10) | data formatting | bytes 2097152
  53.0 0.5 copy.9
  (2 shorter events, 0.0 us)
Async XLA Ops:
  0.6 0.7 %copy-start.1 = (bf16[2048]{0:T(1024)(128)(2,1)S(1)}, bf16[2048]{0:T(1024)(128)(2,1)}, u32[]{:S(2)}) copy-start(bf16[2048]{0:T(1024)(128)(2,1)} %param.7) | copy-start | bytes 12292
  0.6 0.7 %copy-start.2 = (bf16[2048]{0:T(1024)(128)(2,1)S(1)}, bf16[2048]{0:T(1024)(128)(2,1)}, u32[]{:S(2)}) copy-start(bf16[2048]{0:T(1024)(128)(2,1)} %param.6) | copy-start | bytes 12292
  1.4 1.0 %copy-start = (s32[32,2048]{1,0:T(8,128)S(1)}, s32[32,2048]{1,0:T(8,128)}, u32[]{:S(2)}) copy-start(s32[32,2048]{1,0:T(8,128)} %bins_hbm.1) | copy-start | bytes 786436
